TPU v7x, 256 devices: a whole 4x4x8 slice. The times are simulated.
256 devices in a mesh: dp: 32 (over z, y), tensor: 8 (over x, core).
Axes of the slice: x: 4, y: 4, z: 8, core: 2. Of those that a mesh axis runs over, the one named last changes fastest.
Arguments:
- saved_inputs: bfloat16 [2, 65536, 3584], P(None, 'dp'), may hold values from -6 to 6
- kv_cotangent: bfloat16 [2, 65536, 2048], P(None, 'dp', 'tensor'), may hold values from -0.125 to 0.125
- error_buffer: bfloat16 [32, 2, 3584, 2048], P('dp', None, None, 'tensor'), may hold values from -3 to 3
- q_start: float32 [2, 32, 2048], P(None, None, 'tensor'), may hold values from -0.125 to 0.125
Outputs:
- new_error: bfloat16 [32, 2, 3584, 2048], P('dp', None, None, 'tensor')
- q_factor: float32 [2, 32, 2048], P(None, None, 'tensor')
All inputs are finite; a program needn't handle non-finite values.
Results may differ from a plain program's by a relative error of at most 0.001.
Values sent between devices are 32-bit elements; how exact they have to be, the bound alone decides.
A program may use at most 128 MiB of HBM per device.

v0:
```python
import jax
import jax.numpy as jnp
from jax import lax
from jax.sharding import PartitionSpec as P

highest_precision = lax.Precision.HIGHEST


def gram_matrix_of(factor_matrix):
    return jnp.einsum("nrf,nsf->nrs", factor_matrix, factor_matrix, precision=highest_precision)


def compress_factors(merged, q_start):
    p_term = jnp.einsum("nrc,nfc->nrf", q_start, merged, precision=highest_precision)
    p_full = lax.psum(p_term, ("dp", "tensor"))
    lower_factor = jnp.linalg.cholesky(gram_matrix_of(p_full))
    ortho_factor = lax.linalg.triangular_solve(lower_factor, p_full, left_side=True, lower=True)
    q_part = jnp.einsum("nrf,nfc->nrc", ortho_factor, merged, precision=highest_precision)
    q_mean = lax.psum(q_part, "dp") / lax.axis_size("dp")
    decompressed = jnp.einsum("nrf,nrc->nfc", ortho_factor, q_mean, precision=highest_precision)
    return (q_mean, (merged - decompressed).astype(jnp.bfloat16))


def body(saved_inputs, kv_cotangent, error_buffer, q_start):
    layer_count = saved_inputs.shape[0]
    q_parts = [None] * layer_count
    error_parts = [None] * layer_count
    for layer_index in reversed(range(layer_count)):
        weight_gradient = jnp.dot(
            saved_inputs[layer_index].T,
            kv_cotangent[layer_index],
            preferred_element_type=jnp.float32,
        )
        q_mean, fresh_error = compress_factors(
            (weight_gradient + error_buffer[0, layer_index].astype(jnp.float32))[None],
            q_start[layer_index][None],
        )
        q_parts[layer_index] = q_mean
        error_parts[layer_index] = fresh_error
    q_factor = jnp.concatenate(q_parts, axis=0)
    new_error = jnp.concatenate(error_parts, axis=0)
    return (new_error[None], q_factor)


def solution(mesh):
    placed = (
        P(None, "dp", None),
        P(None, "dp", "tensor"),
        P("dp", None, None, "tensor"),
        P(None, None, "tensor"),
    )
    return jax.shard_map(
        body,
        mesh=mesh,
        in_specs=placed,
        out_specs=(P("dp", None, None, "tensor"), P(None, None, "tensor")),
        check_vma=False,
    )
```

profile of v0, /device:TPU:8, one launch (start us, length us, event | category | flops | bytes accessed | tf_op | source)
XLA Modules:
  0.0 475.5 jit_solution(9157769008436325714)
XLA Ops:
  7.2 10.4 %fusion.9 = f32[3584,256]{1,0:T(8,128)S(1)} fusion(bf16[2,2048,3584]{2,1,0:T(8,128)(2,1)} %param.7, bf16[1,2,3584,256]{3,2,1,0:T(8,128)(2,1)} %param.9, bf16[2,2048,256]{2,1,0:T(8,128)(2,1)} %param.8), kind=kOutput, calls=%fused_computation.9 | convolution fusion | flops 3759931392 | bytes 21233664 | tf_op jit(solution)/shard_map/dot_general | solution.py:29
  17.7 9.0 %fusion.6 = f32[3584,256]{1,0:T(8,128)S(1)} fusion(bf16[2,2048,3584]{2,1,0:T(8,128)(2,1)} %param.7, bf16[1,2,3584,256]{3,2,1,0:T(8,128)(2,1)S(1)} %copy-done.7, bf16[2,2048,256]{2,1,0:T(8,128)(2,1)S(1)} %copy-done.8), kind=kOutput, calls=%fused_computation.8 | convolution fusion | flops 3759931392 | bytes 21233664 | tf_op jit(solution)/shard_map/dot_general | solution.py:29
  26.7 4.2 convolution_bitcast_fusion
  31.0 4.2 convolution_bitcast_fusion.1
  35.5 257.7 %all-reduce.5.cloned.1.call-done = (f32[1,32,3584]{2,1,0:T(8,128)}, f32[1,32,3584]{2,1,0:T(8,128)}) async-done(((f32[1,32,3584]{2,1,0:T(8,128)}, f32[1,32,3584]{2,1,0:T(8,128)}), (f32[1,32,3584]{2,1,0:T(8,128)}, f32[1,32,3584]{2,1,0:T(8,128)})) %all-reduce.5.cloned.1.call-update) | async-done | bytes 917520 | tf_op jit(solution)/shard_map/psum | solution.py:15
  293.2 1.7 fusion.22
  294.9 1.7 fusion.26
  296.6 2.9 custom-call.8
  299.6 0.6 compare_reduce_fusion.1
  300.2 0.7 fusion.34
  300.9 2.4 custom-call.9
  303.3 1.6 fusion.24
  305.0 2.9 custom-call.10
  308.0 0.6 compare_reduce_fusion
  308.6 0.7 fusion.35
  309.3 2.4 custom-call.11
  311.7 1.8 fusion.20
  313.5 4.5 convolution_bitcast_fusion.2
  318.0 2.5 convolution_bitcast_fusion.3
  320.5 137.2 %all-reduce.7.cloned.1.call-done = (f32[1,32,256]{2,1,0:T(8,128)}, f32[1,32,256]{2,1,0:T(8,128)}) async-done(((f32[1,32,256]{2,1,0:T(8,128)}, f32[1,32,256]{2,1,0:T(8,128)}), (f32[1,32,256]{2,1,0:T(8,128)}, f32[1,32,256]{2,1,0:T(8,128)})) %all-reduce.7.cloned.1.call-update) | async-done | bytes 65552 | tf_op jit(solution)/shard_map/psum | solution.py:19
  457.7 5.0 %fusion.15 = bf16[1,3584,256]{2,1,0:T(8,128)(2,1)S(1)} fusion(f32[3584,256]{1,0:T(8,128)} %copy-done.2, f32[32,3584]{1,0:T(8,128)S(1)} %fusion.24, f32[1,32,256]{2,1,0:T(8,128)} %get-tuple-element.7), kind=kOutput, calls=%fused_computation.13 | convolution fusion | flops 354164736 | bytes 5996544 | tf_op jit(solution)/shard_map/nrf,nrc->nfc/dot_general | solution.py:20
  462.7 3.1 fusion.14
  465.9 2.2 maximum_bitcast_fusion
  468.0 0.6 pad_maximum_fusion
  (29 shorter events, 0.6 us)
Async XLA Ops:
  7.2 10.5 %copy-start.8 = (bf16[2,2048,256]{2,1,0:T(8,128)(2,1)S(1)}, bf16[2,2048,256]{2,1,0:T(8,128)(2,1)}, u32[]{:S(2)}) copy-start(bf16[2,2048,256]{2,1,0:T(8,128)(2,1)} %param.8) | copy-start | bytes 6291460
  7.2 286.0 %all-reduce.5.cloned.1.call-start = ((), (), s32[]{:S(2)}) async-start(), calls=%async_computation | async-start | bytes 1835008 | tf_op jit(solution)/shard_map/psum | solution.py:15
  7.2 10.4 %copy-start.7 = (bf16[1,2,3584,256]{3,2,1,0:T(8,128)(2,1)S(1)}, bf16[1,2,3584,256]{3,2,1,0:T(8,128)(2,1)}, u32[]{:S(2)}) copy-start(bf16[1,2,3584,256]{3,2,1,0:T(8,128)(2,1)} %param.9) | copy-start | bytes 11010052
  17.6 9.1 %copy-start = (f32[3584,256]{1,0:T(8,128)}, f32[3584,256]{1,0:T(8,128)S(1)}, u32[]{:S(2)}) copy-start(f32[3584,256]{1,0:T(8,128)S(1)} %fusion.9) | copy-start | bytes 11010052
  17.6 9.1 %copy-start.6 = (f32[2,32,256]{2,1,0:T(8,128)S(1)}, f32[2,32,256]{2,1,0:T(8,128)}, u32[]{:S(2)}) copy-start(f32[2,32,256]{2,1,0:T(8,128)} %param.10) | copy-start | bytes 196612
  26.7 4.3 copy-start.2
  35.2 422.5 %all-reduce.7.cloned.1.call-start = ((), (), s32[]{:S(2)}) async-start(), calls=%async_computation.1 | async-start | bytes 131072 | tf_op jit(solution)/shard_map/psum | solution.py:19
  311.7 6.3 %copy-start.3 = (f32[3584,256]{1,0:T(8,128)S(1)}, f32[3584,256]{1,0:T(8,128)}, u32[]{:S(2)}) copy-start(f32[3584,256]{1,0:T(8,128)} %copy-done.2) | copy-start | bytes 11010052
  457.7 5.0 %copy-start.1 = (f32[3584,256]{1,0:T(8,128)S(1)}, f32[3584,256]{1,0:T(8,128)}, u32[]{:S(2)}) copy-start(f32[3584,256]{1,0:T(8,128)} %copy-done) | copy-start | bytes 11010052
  457.7 5.0 %copy-start.4 = (f32[1,32,256]{2,1,0:T(8,128)S(1)}, f32[1,32,256]{2,1,0:T(8,128)}, u32[]{:S(2)}) copy-start(f32[1,32,256]{2,1,0:T(8,128)} %get-tuple-element.6) | copy-start | bytes 98308
  462.7 3.1 copy-start.5
Sparse Core Ops, SparseCore 0:
  35.4 257.8 all-reduce.4
  320.6 137.0 all-reduce.6
where the time goes:
time: 476 us
  waiting for transfers between devices  395 us (83%)
  matrix products  49.7 us (10%)
  other arithmetic  16.2 us (3%)
  between operations  14.2 us (3%)
    psum x1, waiting for transfers between devices, compress_factors(): p_full = lax.psum(p_term, ('dp', 'tensor'))  258 us
    psum x1, waiting for transfers between devices, compress_factors(): q_mean = lax.psum(q_part, 'dp') / lax.axis_size('dp')  137 us
    dot_general x2, matrix products, body(): jnp.dot(saved_inputs[layer_index].T, kv_cotangent[layer_index], preferred...  19.4 us
  transfers between devices with their start and end apart: 2, of which 2 were waited for; matrix products, arithmetic and copies ran while one was open for 0% of the time, Pallas kernels for 0%

commit v1 on v0

v1 whole, which is shorter than its diff:
```python
import functools

import jax
import jax.numpy as jnp
from jax import lax
from jax.experimental import pallas as pl
from jax.experimental.pallas import tpu as pltpu
from jax.sharding import PartitionSpec as P

MESH = pl.DeviceIdType.MESH
F32, BF16 = jnp.float32, jnp.bfloat16
FEATS, RANK, LAYERS, TOK, COLS = 3584, 32, 2, 2048, 256
NZ, NY, NX = 8, 4, 4
HALF = TOK // 2
BLK = 128
NBLK = FEATS // BLK
OWN = NBLK // 2
GRAD_F = 512


def mm(a, b, ca=1, cb=0, precision=None):
    return lax.dot_general(a, b, (((ca,), (cb,)), ((), ())), precision=precision, preferred_element_type=F32)


def split3(v):
    hi = v.astype(BF16)
    rest = v - hi.astype(F32)
    mid = rest.astype(BF16)
    lo = (rest - mid.astype(F32)).astype(BF16)
    return jnp.concatenate([hi, mid, lo], axis=0)


def fold3(r):
    return r[0:RANK] + r[RANK : 2 * RANK] + r[2 * RANK : 3 * RANK]


def kernel(
    s_hbm, k_hbm, e_hbm, q_hbm, err_hbm, qf_hbm,
    s, k, e, qv, q3, m, hi, lo, ot, zl, zr, z3, pp, cr, ps, xr, zs, pf, gl, ub, yr, zq, qt, qo,
    hs, out_sem, z_s, z_r, c_s, c_r, xy_s, xy_r, zz_s, zz_r, ag_s, ag_r, ac_s, ac_r, y1_s, y1_r, qz_s, qz_r, y2_s, y2_r,
):
    dp, t = lax.axis_index("dp"), lax.axis_index("tensor")
    z, y, x, c = dp // NY, dp % NY, t // 2, t % 2
    xy = y * NX + x

    def dev(z_, y_, x_, c_):
        return (z_ * NY + y_, x_ * 2 + c_)

    partner = dev(z, y, x, 1 - c)

    def xy_peer(j):
        return (y + j // NX) % NY, (x + j % NX) % NX

    def remote(src, dst, ss, rs, device):
        return pltpu.make_async_remote_copy(
            src_ref=src, dst_ref=dst, send_sem=ss, recv_sem=rs, device_id=device, device_id_type=MESH
        )

    def wait_recv(ref, ss, rs):
        remote(ref, ref, ss, rs, partner).wait_recv()

    def wait_send(ref, ss, rs):
        remote(ref, ref, ss, rs, partner).wait_send()

    barrier = pltpu.get_barrier_semaphore()
    pl.semaphore_signal(barrier, inc=1, device_id=partner, device_id_type=MESH)

    def greet_z(j, _):
        pl.semaphore_signal(barrier, inc=1, device_id=dev((z + j) % NZ, y, x, c), device_id_type=MESH)
        return 0

    def greet_xy(j, _):
        ny, nx = xy_peer(j)
        pl.semaphore_signal(barrier, inc=1, device_id=dev(z, ny, nx, c), device_id_type=MESH)
        return 0

    lax.fori_loop(1, NZ, greet_z, 0)
    lax.fori_loop(1, NX * NY, greet_xy, 0)

    def half_copy(hbm, vmem, l, part, sem):
        rows = pl.ds(pl.multiple_of((c if part == 0 else 1 - c) * HALF, HALF), HALF)
        return pltpu.make_async_copy(hbm.at[l, rows], vmem.at[l, pl.ds(part * HALF, HALF)], sem)

    cq = pltpu.make_async_copy(q_hbm, qv, hs.at[0])
    ck = [[half_copy(k_hbm, k, l, h, hs.at[1 + 2 * l + h]) for h in range(2)] for l in range(LAYERS)]
    ce = [pltpu.make_async_copy(e_hbm.at[0, l], e.at[l], hs.at[5 + l]) for l in range(LAYERS)]
    cs = [[half_copy(s_hbm, s, l, h, hs.at[7 + 2 * l + h]) for h in range(2)] for l in range(LAYERS)]
    cq.start()
    for l in range(LAYERS):
        ck[l][0].start()
        ck[l][1].start()
    ce[0].start()
    ce[1].start()
    cs[0][0].start()

    cq.wait()
    for l in range(LAYERS):
        q3[l] = split3(qv[l])
    for l in range(LAYERS):
        ck[l][0].wait()
        ck[l][1].wait()
        for h in range(2):
            zl[l, h] = fold3(mm(q3[l], k[l, pl.ds(h * HALF, HALF), :], 1, 1))
    cs[1][0].start()

    def error_part(l):
        def step(i, _):
            r = fold3(mm(q3[l], e[l, pl.ds(pl.multiple_of(i * 512, 512), 512), :], 1, 1))
            for j in range(4):
                pp[l, i * 4 + j] = r[:, j * BLK : (j + 1) * BLK]
            return 0

        ce[l].wait()
        lax.fori_loop(0, FEATS // 512, step, 0)

    error_part(0)

    pl.semaphore_wait(barrier, 1 + (NZ - 1) + (NX * NY - 1))
    for l in range(LAYERS):
        remote(zl.at[l, 1], zr.at[l], z_s.at[l], z_r.at[l], partner).start()
    error_part(1)
    cs[0][1].start()
    cs[1][1].start()

    def p_blocks(l, side):
        def step(i, _):
            b0 = side * OWN + i * 7
            f0 = pl.multiple_of(b0 * BLK, BLK)
            r = fold3(mm(z3[l], s[l, pl.ds(0, HALF), pl.ds(f0, 7 * BLK)]))
            for j in range(7):
                pp[l, b0 + j] += r[:, j * BLK : (j + 1) * BLK]
            return 0

        lax.fori_loop(0, 2, step, 0)

    def p_term(l):
        wait_recv(zr.at[l], z_s.at[l], z_r.at[l])
        z3[l] = split3(zl[l, 0] + zr[l])
        cs[l][0].wait()
        p_blocks(l, 1 - c)
        remote(pp.at[l, pl.ds((1 - c) * OWN, OWN)], cr.at[l], c_s.at[l], c_r.at[l], partner).start()
        p_blocks(l, c)

    def add_cores(l):
        wait_recv(cr.at[l], c_s.at[l], c_r.at[l])

        def step(b, _):
            ps[l, b] = pp[l, c * OWN + b] + cr[l, b]
            return 0

        lax.fori_loop(0, OWN, step, 0)

        def send(j, _):
            ny, nx = xy_peer(j)
            b = ny * NX + nx - 2 * l

            @pl.when((b >= 0) & (b < OWN))
            def _():
                remote(ps.at[l, b], xr.at[l, j - 1], xy_s.at[l], xy_r.at[l], dev(z, ny, nx, c)).start()

            return 0

        lax.fori_loop(1, NX * NY, send, 0)

    def mine(l):
        return xy - 2 * l

    def owner(l):
        return (mine(l) >= 0) & (mine(l) < OWN)

    def add_plane(l):
        @pl.when(owner(l))
        def _():
            wait_recv(xr.at[l], xy_s.at[l], xy_r.at[l])
            total = ps[l, mine(l)]
            for j in range(NX * NY - 1):
                total = total + xr[l, j]
            zs[l, z] = total

            def send(j, _):
                remote(zs.at[l, z], zs.at[l, z], zz_s.at[l], zz_r.at[l], dev((z + j) % NZ, y, x, c)).start()
                return 0

            lax.fori_loop(1, NZ, send, 0)

    def add_z(l):
        @pl.when(owner(l))
        def _():
            wait_recv(zs.at[l, pl.ds(0, NZ - 1)], zz_s.at[l], zz_r.at[l])
            total = zs[l, 0]
            for j in range(1, NZ):
                total = total + zs[l, j]
            b = c * OWN + mine(l)
            pf[l, b] = total

            def send(j, _):
                ny, nx = xy_peer(j)
                remote(pf.at[l, b], pf.at[l, b], ag_s.at[l], ag_r.at[l], dev(z, ny, nx, c)).start()
                return 0

            lax.fori_loop(1, NX * NY, send, 0)

    def share_core(l):
        @pl.when(owner(l))
        def _():
            wait_recv(pf.at[l, pl.ds(0, OWN - 1)], ag_s.at[l], ag_r.at[l])

        @pl.when(jnp.logical_not(owner(l)))
        def _():
            wait_recv(pf.at[l, pl.ds(0, OWN)], ag_s.at[l], ag_r.at[l])

        half = pf.at[l, pl.ds(c * OWN, OWN)]
        remote(half, half, ac_s.at[l], ac_r.at[l], partner).start()

    def grad(l, i0, i1):
        def step(i, _):
            rows = pl.ds(pl.multiple_of(i * GRAD_F, GRAD_F), GRAD_F)
            g = mm(s[l, :, rows], k[l], 0, 0) + e[l, rows, :].astype(F32)
            m[l, rows, :] = g
            top = g.astype(BF16)
            hi[l, rows, :] = top
            lo[l, rows, :] = (g - top.astype(F32)).astype(BF16)
            return 0

        lax.fori_loop(i0, i1, step, 0)

    def q_term(l):
        wait_recv(pf.at[l, pl.ds(0, OWN)], ac_s.at[l], ac_r.at[l])

        def step(i, acc):
            rows = pl.ds(pl.multiple_of(i * 512, 512), 512)
            p3 = split3(jnp.concatenate([pf[l, i * 4 + j] for j in range(4)], axis=1))
            r = fold3(mm(p3, hi[l, rows, :]))
            r2 = mm(p3[0 : 2 * RANK], lo[l, rows, :])
            return acc + (r + (r2[0:RANK] + r2[RANK : 2 * RANK]))

        u = lax.fori_loop(0, FEATS // 512, step, jnp.zeros((RANK, COLS), F32))
        for i in range(NY):
            ub[l, i] = u[8 * i : 8 * i + 8]

        def send(j, _):
            ny = (y + j) % NY
            remote(ub.at[l, ny], yr.at[l, j - 1], y1_s.at[l], y1_r.at[l], dev(z, ny, x, c)).start()
            return 0

        lax.fori_loop(1, NY, send, 0)

    def q_add_y(l):
        wait_recv(yr.at[l], y1_s.at[l], y1_r.at[l])
        zq[l, z] = ub[l, y] + yr[l, 0] + yr[l, 1] + yr[l, 2]

        def send(j, _):
            remote(zq.at[l, z], zq.at[l, z], qz_s.at[l], qz_r.at[l], dev((z + j) % NZ, y, x, c)).start()
            return 0

        lax.fori_loop(1, NZ, send, 0)

    def q_add_z(l):
        wait_recv(zq.at[l, pl.ds(0, NZ - 1)], qz_s.at[l], qz_r.at[l])
        total = zq[l, 0]
        for j in range(1, NZ):
            total = total + zq[l, j]
        qt[l, y] = total * (1.0 / (NZ * NY))

        def send(j, _):
            remote(qt.at[l, y], qt.at[l, y], y2_s.at[l], y2_r.at[l], dev(z, (y + j) % NY, x, c)).start()
            return 0

        lax.fori_loop(1, NY, send, 0)

    def gram(l):
        def step(i, acc):
            p3 = split3(jnp.concatenate([pf[l, i * 4 + j] for j in range(4)], axis=1))
            return acc + mm(p3, p3, 1, 1)

        g = lax.fori_loop(0, FEATS // 512, step, jnp.zeros((3 * RANK, 3 * RANK), F32))
        g = fold3(g)
        return g[:, 0:RANK] + g[:, RANK : 2 * RANK] + g[:, 2 * RANK : 3 * RANK]

    def inverse_factors(grams):
        rows = lax.broadcasted_iota(jnp.int32, (RANK, 1), 0)
        eye = (rows == lax.broadcasted_iota(jnp.int32, (RANK, RANK), 1)).astype(F32)
        work = [jnp.concatenate([g, eye], axis=1) for g in grams]
        for j in range(RANK):
            for n, a in enumerate(work):
                inv = lax.rsqrt(a[j : j + 1, j : j + 1])
                row = a[j : j + 1, :] * inv
                col = jnp.where(rows > j, a[:, j : j + 1] * inv, 0.0)
                work[n] = jnp.where(rows == j, row, a - col * row)
        return [a[:, RANK : 2 * RANK] for a in work]

    def ortho(l):
        def step(i, _):
            o = mm(gl[l], pf[l, i], precision=lax.Precision.HIGHEST)
            top = o.astype(BF16).astype(F32)
            rest = o - top
            wide = jnp.concatenate([top, top, rest, rest], axis=0)
            ot[l, pl.ds(pl.multiple_of(i * BLK, BLK), BLK), :] = wide.T.astype(BF16)
            return 0

        lax.fori_loop(0, NBLK, step, 0)

    def finish(l):
        wait_recv(qt.at[l, pl.ds(0, NY - 1)], y2_s.at[l], y2_r.at[l])
        u = jnp.concatenate([qt[l, i] for i in range(NY)], axis=0)
        q = mm(gl[l], u, precision=lax.Precision.HIGHEST)
        qo[l] = q
        top = q.astype(BF16)
        rest = (q - top.astype(F32)).astype(BF16)
        q4 = jnp.concatenate([top, rest, top, rest], axis=0)

        def step(i, _):
            rows = pl.ds(pl.multiple_of(i * 896, 896), 896)
            e[l, rows, :] = (m[l, rows, :] - mm(ot[l, rows, :], q4)).astype(BF16)
            return 0

        for part in range(2):
            lax.fori_loop(2 * part, 2 * part + 2, step, 0)
            rows = pl.ds(part * 1792, 1792)
            pltpu.make_async_copy(e.at[l, rows], err_hbm.at[0, l, rows], out_sem.at[2 * l + part]).start()

    p_term(0)
    add_cores(0)
    p_term(1)
    add_cores(1)
    cs[0][1].wait()
    grad(0, 0, 5)
    add_plane(0)
    grad(0, 5, 7)
    add_plane(1)
    cs[1][1].wait()
    grad(1, 0, 4)
    add_z(0)
    grad(1, 4, 7)
    add_z(1)
    share_core(0)
    q_term(0)
    g0 = gram(0)
    share_core(1)
    q_term(1)
    q_add_y(0)
    g1 = gram(1)
    q_add_y(1)
    inverses = inverse_factors([g0, g1])
    for l in range(LAYERS):
        gl[l] = inverses[l]
    q_add_z(0)
    ortho(0)
    q_add_z(1)
    ortho(1)
    finish(0)
    finish(1)
    out_q = pltpu.make_async_copy(qo, qf_hbm, out_sem.at[4])
    out_q.start()

    for l in range(LAYERS):
        wait_send(zl.at[l, 1], z_s.at[l], z_r.at[l])
        wait_send(cr.at[l], c_s.at[l], c_r.at[l])

        @pl.when(owner(l))
        def _():
            wait_send(ps.at[l, pl.ds(0, OWN - 1)], xy_s.at[l], xy_r.at[l])
            wait_send(zs.at[l, pl.ds(0, NZ - 1)], zz_s.at[l], zz_r.at[l])
            wait_send(pf.at[l, pl.ds(0, NX * NY - 1)], ag_s.at[l], ag_r.at[l])

        @pl.when(jnp.logical_not(owner(l)))
        def _():
            wait_send(ps.at[l, pl.ds(0, OWN)], xy_s.at[l], xy_r.at[l])

        wait_send(pf.at[l, pl.ds(0, OWN)], ac_s.at[l], ac_r.at[l])
        wait_send(ub.at[l, pl.ds(0, NY - 1)], y1_s.at[l], y1_r.at[l])
        wait_send(zq.at[l, pl.ds(0, NZ - 1)], qz_s.at[l], qz_r.at[l])
        wait_send(qt.at[l, pl.ds(0, NY - 1)], y2_s.at[l], y2_r.at[l])
        for part in range(2):
            rows = pl.ds(part * 1792, 1792)
            pltpu.make_async_copy(e.at[l, rows], err_hbm.at[0, l, rows], out_sem.at[2 * l + part]).wait()
    out_q.wait()


def body(saved_inputs, kv_cotangent, error_buffer, q_start):
    L = LAYERS
    pair = pltpu.SemaphoreType.DMA((L,))
    return pl.pallas_call(
        kernel,
        out_shape=(
            jax.ShapeDtypeStruct((1, L, FEATS, COLS), BF16),
            jax.ShapeDtypeStruct((L, RANK, COLS), F32),
        ),
        in_specs=[pl.BlockSpec(memory_space=pl.ANY)] * 4,
        out_specs=(pl.BlockSpec(memory_space=pl.ANY), pl.BlockSpec(memory_space=pl.ANY)),
        scratch_shapes=[
            pltpu.VMEM((L, TOK, FEATS), BF16),
            pltpu.VMEM((L, TOK, COLS), BF16),
            pltpu.VMEM((L, FEATS, COLS), BF16),
            pltpu.VMEM((L, RANK, COLS), F32),
            pltpu.VMEM((L, 3 * RANK, COLS), BF16),
            pltpu.VMEM((L, FEATS, COLS), F32),
            pltpu.VMEM((L, FEATS, COLS), BF16),
            pltpu.VMEM((L, FEATS, COLS), BF16),
            pltpu.VMEM((L, FEATS, 128), BF16),
            pltpu.VMEM((L, 2, RANK, HALF), F32),
            pltpu.VMEM((L, RANK, HALF), F32),
            pltpu.VMEM((L, 3 * RANK, HALF), BF16),
            pltpu.VMEM((L, NBLK, RANK, BLK), F32),
            pltpu.VMEM((L, OWN, RANK, BLK), F32),
            pltpu.VMEM((L, OWN, RANK, BLK), F32),
            pltpu.VMEM((L, NX * NY - 1, RANK, BLK), F32),
            pltpu.VMEM((L, NZ, RANK, BLK), F32),
            pltpu.VMEM((L, NBLK, RANK, BLK), F32),
            pltpu.VMEM((L, RANK, RANK), F32),
            pltpu.VMEM((L, NY, 8, COLS), F32),
            pltpu.VMEM((L, NY - 1, 8, COLS), F32),
            pltpu.VMEM((L, NZ, 8, COLS), F32),
            pltpu.VMEM((L, NY, 8, COLS), F32),
            pltpu.VMEM((L, RANK, COLS), F32),
            pltpu.SemaphoreType.DMA((11,)),
            pltpu.SemaphoreType.DMA((5,)),
        ]
        + [pair] * 18,
        compiler_params=pltpu.CompilerParams(
            collective_id=0, has_side_effects=True, vmem_limit_bytes=60 * 1024 * 1024
        ),
        cost_estimate=pl.CostEstimate(flops=8_600_000_000, bytes_accessed=39_000_000, transcendentals=0),
    )(saved_inputs, kv_cotangent, error_buffer, q_start)


def solution(mesh):
    placed = (
        P(None, "dp", None),
        P(None, "dp", "tensor"),
        P("dp", None, None, "tensor"),
        P(None, None, "tensor"),
    )
    return jax.shard_map(
        body,
        mesh=mesh,
        in_specs=placed,
        out_specs=(P("dp", None, None, "tensor"), P(None, None, "tensor")),
        check_vma=False,
    )
```

time: 476 us -> 70.8 us (0.15)
  waiting for transfers between devices: 395 us -> 0 us
  Pallas kernels: 0 us -> 64.9 us
  matrix products: 49.7 us -> 0 us
  other arithmetic: 16.2 us -> 0 us
  between operations: 14.2 us -> 0.65 us
    psum x2 -> x0, waiting for transfers between devices: 395 us -> none  [the longest x1 258 us: compress_factors(): p_full = lax.psum(p_term, ('dp', 'tensor'))]
    pallas_call x0 -> x1, Pallas kernels: none -> 64.9 us  [body(): pl.pallas_call(kernel, out_shape=(jax.ShapeDtypeStruct((1, L, FEATS, COLS...]
    dot_general x10 -> x0, matrix products: 46.3 us -> none  [the longest x2 19.4 us: body(): jnp.dot(saved_inputs[layer_index].T, kv_cotangent[layer_index], preferred...]
    another operation x10 -> x0, other arithmetic: 13.4 us -> none  [the longest x6 7.19 us: compress_factors(): lower_factor = jnp.linalg.cholesky(gram_matrix_of(p_full))]
  transfers between devices with their start and end apart: 2 -> 0, of which waited for: 2 -> 0; matrix products, arithmetic and copies ran while one was open for 0% -> 0% of each run, Pallas kernels for 0% -> 0%
where the time goes in v1:
time: 70.8 us; the launch traced here: 70.4 us
  Pallas kernels  64.9 us (92%)
  local copies, waits for them, and re-layouts  4.78 us (7%)
    pallas_call x1, Pallas kernels, body(): pl.pallas_call(kernel, out_shape=(jax.ShapeDtypeStruct((1, L, FEATS, COLS...  64.9 us
    unnamed x4, local copies, waits for them, and re-layouts  4.78 us

profile of v1, /device:TPU:8, one launch (start us, length us, event | category | flops | bytes accessed | tf_op | source)
XLA Modules:
  0.0 70.4 jit_solution(3064453278467938803)
XLA Ops:
  0.6 64.9 %shard_map.59 = (bf16[1,2,3584,256]{3,2,1,0:T(8,128)(2,1)}, f32[2,32,256]{2,1,0:T(8,128)}) custom-call(bf16[2,2048,3584]{2,1,0:T(8,128)(2,1)} %s_hbm.1, bf16[2,2048,256]{2,1,0:T(8,128)(2,1)} %k_hbm.1, bf16[1,2,3584,256]{3,2,1,0:T(8,128)(2,1)} %e_hbm.1, f32[2,32,256]{2,1,0:T(8,128)} %q_hbm.1), custom_call_target="tpu_custom_call" | custom-call | flops 8600000512 | bytes 39000000 | tf_op jit(solution)/shard_map/pallas_call | solution.py:383
  65.6 0.0 copy-start
  65.6 4.1 %copy.8 = bf16[1,2,3584,256]{3,2,1,0:T(8,128)(2,1)} copy(bf16[1,2,3584,256]{3,2,1,0:T(8,128)(2,1)} %get-tuple-element.4) | data formatting | bytes 7340032
  69.7 0.0 copy-done
  69.7 0.6 copy.9
Async XLA Ops:
  65.6 4.2 %copy-start = (f32[2,32,256]{2,1,0:T(8,128)S(1)}, f32[2,32,256]{2,1,0:T(8,128)}, u32[]{:S(2)}) copy-start(f32[2,32,256]{2,1,0:T(8,128)} %get-tuple-element.5) | copy-start | bytes 196612

commit v2 on v1

--- a/solution.py
+++ b/solution.py
@@ -35,9 +35,9 @@
 
 
 def kernel(
-    s_hbm, k_hbm, e_hbm, q_hbm, err_hbm, qf_hbm,
-    s, k, e, qv, q3, m, hi, lo, ot, zl, zr, z3, pp, cr, ps, xr, zs, pf, gl, ub, yr, zq, qt, qo,
-    hs, out_sem, z_s, z_r, c_s, c_r, xy_s, xy_r, zz_s, zz_r, ag_s, ag_r, ac_s, ac_r, y1_s, y1_r, qz_s, qz_r, y2_s, y2_r,
+    s_hbm, k_hbm, e_hbm, q_hbm, m, ot, gl, qt,
+    s, k, e, qv, q3, hi, lo, zl, zr, z3, pp, cr, ps, xr, zs, pf, p3, ub, yr, zq,
+    hs, z_s, z_r, c_s, c_r, xy_s, xy_r, zz_s, zz_r, ag_s, ag_r, ac_s, ac_r, y1_s, y1_r, qz_s, qz_r, y2_s, y2_r,
 ):
     dp, t = lax.axis_index("dp"), lax.axis_index("tensor")
     z, y, x, c = dp // NY, dp % NY, t // 2, t % 2
@@ -77,21 +77,23 @@
     lax.fori_loop(1, NZ, greet_z, 0)
     lax.fori_loop(1, NX * NY, greet_xy, 0)
 
-    def half_copy(hbm, vmem, l, part, sem):
-        rows = pl.ds(pl.multiple_of((c if part == 0 else 1 - c) * HALF, HALF), HALF)
-        return pltpu.make_async_copy(hbm.at[l, rows], vmem.at[l, pl.ds(part * HALF, HALF)], sem)
+    def token_copy(hbm, vmem, l, part, first, count, sem):
+        rows = pl.ds(pl.multiple_of((c if part == 0 else 1 - c) * HALF + first, count), count)
+        return pltpu.make_async_copy(hbm.at[l, rows], vmem.at[l, pl.ds(part * HALF + first, count)], sem)
 
     cq = pltpu.make_async_copy(q_hbm, qv, hs.at[0])
-    ck = [[half_copy(k_hbm, k, l, h, hs.at[1 + 2 * l + h]) for h in range(2)] for l in range(LAYERS)]
+    ck = [[token_copy(k_hbm, k, l, h, 0, HALF, hs.at[1 + 2 * l + h]) for h in range(2)] for l in range(LAYERS)]
     ce = [pltpu.make_async_copy(e_hbm.at[0, l], e.at[l], hs.at[5 + l]) for l in range(LAYERS)]
-    cs = [[half_copy(s_hbm, s, l, h, hs.at[7 + 2 * l + h]) for h in range(2)] for l in range(LAYERS)]
+    own = [
+        [token_copy(s_hbm, s, l, 0, i * HALF // 2, HALF // 2, hs.at[7 + 2 * l + i]) for i in range(2)] for l in range(LAYERS)
+    ]
+    rest = [token_copy(s_hbm, s, l, 1, 0, HALF, hs.at[11 + l]) for l in range(LAYERS)]
     cq.start()
     for l in range(LAYERS):
         ck[l][0].start()
         ck[l][1].start()
     ce[0].start()
     ce[1].start()
-    cs[0][0].start()
 
     cq.wait()
     for l in range(LAYERS):
@@ -99,44 +101,44 @@
     for l in range(LAYERS):
         ck[l][0].wait()
         ck[l][1].wait()
+        own[0][l].start()
         for h in range(2):
             zl[l, h] = fold3(mm(q3[l], k[l, pl.ds(h * HALF, HALF), :], 1, 1))
-    cs[1][0].start()
 
     def error_part(l):
-        def step(i, _):
-            r = fold3(mm(q3[l], e[l, pl.ds(pl.multiple_of(i * 512, 512), 512), :], 1, 1))
-            for j in range(4):
-                pp[l, i * 4 + j] = r[:, j * BLK : (j + 1) * BLK]
-            return 0
-
         ce[l].wait()
-        lax.fori_loop(0, FEATS // 512, step, 0)
+        for i in range(4):
+            r = fold3(mm(q3[l], e[l, pl.ds(i * 896, 896), :], 1, 1))
+            for j in range(7):
+                pp[l, i * 7 + j] = r[:, j * BLK : (j + 1) * BLK]
 
     error_part(0)
+    own[1][0].start()
+    error_part(1)
 
     pl.semaphore_wait(barrier, 1 + (NZ - 1) + (NX * NY - 1))
     for l in range(LAYERS):
         remote(zl.at[l, 1], zr.at[l], z_s.at[l], z_r.at[l], partner).start()
-    error_part(1)
-    cs[0][1].start()
-    cs[1][1].start()
 
     def p_blocks(l, side):
-        def step(i, _):
+        for i in range(2):
             b0 = side * OWN + i * 7
             f0 = pl.multiple_of(b0 * BLK, BLK)
             r = fold3(mm(z3[l], s[l, pl.ds(0, HALF), pl.ds(f0, 7 * BLK)]))
             for j in range(7):
                 pp[l, b0 + j] += r[:, j * BLK : (j + 1) * BLK]
-            return 0
-
-        lax.fori_loop(0, 2, step, 0)
 
     def p_term(l):
         wait_recv(zr.at[l], z_s.at[l], z_r.at[l])
         z3[l] = split3(zl[l, 0] + zr[l])
-        cs[l][0].wait()
+        own[l][0].wait()
+        if l == 0:
+            own[1][1].start()
+        else:
+            rest[0].start()
+        own[l][1].wait()
+        if l == 1:
+            rest[1].start()
         p_blocks(l, 1 - c)
         remote(pp.at[l, pl.ds((1 - c) * OWN, OWN)], cr.at[l], c_s.at[l], c_r.at[l], partner).start()
         p_blocks(l, c)
@@ -213,28 +215,24 @@
         remote(half, half, ac_s.at[l], ac_r.at[l], partner).start()
 
     def grad(l, i0, i1):
-        def step(i, _):
-            rows = pl.ds(pl.multiple_of(i * GRAD_F, GRAD_F), GRAD_F)
+        for i in range(i0, i1):
+            rows = pl.ds(i * GRAD_F, GRAD_F)
             g = mm(s[l, :, rows], k[l], 0, 0) + e[l, rows, :].astype(F32)
             m[l, rows, :] = g
             top = g.astype(BF16)
             hi[l, rows, :] = top
             lo[l, rows, :] = (g - top.astype(F32)).astype(BF16)
-            return 0
-
-        lax.fori_loop(i0, i1, step, 0)
 
     def q_term(l):
         wait_recv(pf.at[l, pl.ds(0, OWN)], ac_s.at[l], ac_r.at[l])
-
-        def step(i, acc):
-            rows = pl.ds(pl.multiple_of(i * 512, 512), 512)
-            p3 = split3(jnp.concatenate([pf[l, i * 4 + j] for j in range(4)], axis=1))
-            r = fold3(mm(p3, hi[l, rows, :]))
-            r2 = mm(p3[0 : 2 * RANK], lo[l, rows, :])
-            return acc + (r + (r2[0:RANK] + r2[RANK : 2 * RANK]))
-
-        u = lax.fori_loop(0, FEATS // 512, step, jnp.zeros((RANK, COLS), F32))
+        u = jnp.zeros((RANK, COLS), F32)
+        for i in range(FEATS // 512):
+            rows = pl.ds(i * 512, 512)
+            terms = split3(jnp.concatenate([pf[l, i * 4 + j] for j in range(4)], axis=1))
+            p3[l, :, rows] = terms
+            r = fold3(mm(terms, hi[l, rows, :]))
+            r2 = mm(terms[0 : 2 * RANK], lo[l, rows, :])
+            u = u + (r + (r2[0:RANK] + r2[RANK : 2 * RANK]))
         for i in range(NY):
             ub[l, i] = u[8 * i : 8 * i + 8]
 
@@ -269,11 +267,10 @@
         lax.fori_loop(1, NY, send, 0)
 
     def gram(l):
-        def step(i, acc):
-            p3 = split3(jnp.concatenate([pf[l, i * 4 + j] for j in range(4)], axis=1))
-            return acc + mm(p3, p3, 1, 1)
-
-        g = lax.fori_loop(0, FEATS // 512, step, jnp.zeros((3 * RANK, 3 * RANK), F32))
+        g = jnp.zeros((3 * RANK, 3 * RANK), F32)
+        for i in range(FEATS // 512):
+            terms = p3[l, :, pl.ds(i * 512, 512)]
+            g = g + mm(terms, terms, 1, 1)
         g = fold3(g)
         return g[:, 0:RANK] + g[:, RANK : 2 * RANK] + g[:, 2 * RANK : 3 * RANK]
 
@@ -290,45 +287,27 @@
         return [a[:, RANK : 2 * RANK] for a in work]
 
     def ortho(l):
-        def step(i, _):
-            o = mm(gl[l], pf[l, i], precision=lax.Precision.HIGHEST)
-            top = o.astype(BF16).astype(F32)
-            rest = o - top
-            wide = jnp.concatenate([top, top, rest, rest], axis=0)
-            ot[l, pl.ds(pl.multiple_of(i * BLK, BLK), BLK), :] = wide.T.astype(BF16)
-            return 0
-
-        lax.fori_loop(0, NBLK, step, 0)
-
-    def finish(l):
-        wait_recv(qt.at[l, pl.ds(0, NY - 1)], y2_s.at[l], y2_r.at[l])
-        u = jnp.concatenate([qt[l, i] for i in range(NY)], axis=0)
-        q = mm(gl[l], u, precision=lax.Precision.HIGHEST)
-        qo[l] = q
-        top = q.astype(BF16)
-        rest = (q - top.astype(F32)).astype(BF16)
-        q4 = jnp.concatenate([top, rest, top, rest], axis=0)
-
-        def step(i, _):
-            rows = pl.ds(pl.multiple_of(i * 896, 896), 896)
-            e[l, rows, :] = (m[l, rows, :] - mm(ot[l, rows, :], q4)).astype(BF16)
-            return 0
-
-        for part in range(2):
-            lax.fori_loop(2 * part, 2 * part + 2, step, 0)
-            rows = pl.ds(part * 1792, 1792)
-            pltpu.make_async_copy(e.at[l, rows], err_hbm.at[0, l, rows], out_sem.at[2 * l + part]).start()
+        g3 = split3(gl[l])
+        top, mid, low = g3[0:RANK], g3[RANK : 2 * RANK], g3[2 * RANK : 3 * RANK]
+        left = jnp.concatenate([top, top, top, mid, mid, low], axis=1)
+        for i in range(FEATS // 512):
+            rows = pl.ds(i * 512, 512)
+            p_top, p_mid, p_low = (p3[l, pl.ds(n * RANK, RANK), rows] for n in range(3))
+            o = mm(left, jnp.concatenate([p_top, p_mid, p_low, p_top, p_mid, p_top], axis=0))
+            o_top = o.astype(BF16)
+            o_low = (o - o_top.astype(F32)).astype(BF16)
+            ot[l, rows, :] = jnp.concatenate([o_top, o_top, o_low, o_low], axis=0).T
 
     p_term(0)
     add_cores(0)
     p_term(1)
     add_cores(1)
-    cs[0][1].wait()
-    grad(0, 0, 5)
+    rest[0].wait()
+    grad(0, 0, 4)
     add_plane(0)
-    grad(0, 5, 7)
+    grad(0, 4, 7)
     add_plane(1)
-    cs[1][1].wait()
+    rest[1].wait()
     grad(1, 0, 4)
     add_z(0)
     grad(1, 4, 7)
@@ -348,10 +327,8 @@
     ortho(0)
     q_add_z(1)
     ortho(1)
-    finish(0)
-    finish(1)
-    out_q = pltpu.make_async_copy(qo, qf_hbm, out_sem.at[4])
-    out_q.start()
+    for l in range(LAYERS):
+        wait_recv(qt.at[l, pl.ds(0, NY - 1)], y2_s.at[l], y2_r.at[l])
 
     for l in range(LAYERS):
         wait_send(zl.at[l, 1], z_s.at[l], z_r.at[l])
@@ -371,33 +348,48 @@
         wait_send(ub.at[l, pl.ds(0, NY - 1)], y1_s.at[l], y1_r.at[l])
         wait_send(zq.at[l, pl.ds(0, NZ - 1)], qz_s.at[l], qz_r.at[l])
         wait_send(qt.at[l, pl.ds(0, NY - 1)], y2_s.at[l], y2_r.at[l])
-        for part in range(2):
-            rows = pl.ds(part * 1792, 1792)
-            pltpu.make_async_copy(e.at[l, rows], err_hbm.at[0, l, rows], out_sem.at[2 * l + part]).wait()
-    out_q.wait()
+
+
+def finish(m, ot, gl, qt, err_hbm, qf, out, sems):
+    copies = []
+    for l in range(LAYERS):
+        u = jnp.concatenate([qt[l, i] for i in range(NY)], axis=0)
+        q = mm(gl[l], u, precision=lax.Precision.HIGHEST)
+        qf[l] = q
+        top = q.astype(BF16)
+        rest = (q - top.astype(F32)).astype(BF16)
+        q4 = jnp.concatenate([top, rest, top, rest], axis=0)
+        for i in range(FEATS // 512):
+            rows = pl.ds(i * 512, 512)
+            out[l, rows, :] = (m[l, rows, :] - mm(ot[l, rows, :], q4)).astype(BF16)
+            copies.append(pltpu.make_async_copy(out.at[l, rows], err_hbm.at[0, l, rows], sems.at[len(copies)]))
+            copies[-1].start()
+    for copy in copies:
+        copy.wait()
 
 
 def body(saved_inputs, kv_cotangent, error_buffer, q_start):
     L = LAYERS
     pair = pltpu.SemaphoreType.DMA((L,))
-    return pl.pallas_call(
+    any_spec, vmem_spec = pl.BlockSpec(memory_space=pl.ANY), pl.BlockSpec(memory_space=pltpu.VMEM)
+    held = pl.pallas_call(
         kernel,
         out_shape=(
-            jax.ShapeDtypeStruct((1, L, FEATS, COLS), BF16),
-            jax.ShapeDtypeStruct((L, RANK, COLS), F32),
+            pltpu.VMEM((L, FEATS, COLS), F32),
+            pltpu.VMEM((L, FEATS, 128), BF16),
+            pltpu.VMEM((L, RANK, RANK), F32),
+            pltpu.VMEM((L, NY, 8, COLS), F32),
         ),
-        in_specs=[pl.BlockSpec(memory_space=pl.ANY)] * 4,
-        out_specs=(pl.BlockSpec(memory_space=pl.ANY), pl.BlockSpec(memory_space=pl.ANY)),
+        in_specs=[any_spec] * 4,
+        out_specs=(vmem_spec,) * 4,
         scratch_shapes=[
             pltpu.VMEM((L, TOK, FEATS), BF16),
             pltpu.VMEM((L, TOK, COLS), BF16),
             pltpu.VMEM((L, FEATS, COLS), BF16),
             pltpu.VMEM((L, RANK, COLS), F32),
             pltpu.VMEM((L, 3 * RANK, COLS), BF16),
-            pltpu.VMEM((L, FEATS, COLS), F32),
             pltpu.VMEM((L, FEATS, COLS), BF16),
             pltpu.VMEM((L, FEATS, COLS), BF16),
-            pltpu.VMEM((L, FEATS, 128), BF16),
             pltpu.VMEM((L, 2, RANK, HALF), F32),
             pltpu.VMEM((L, RANK, HALF), F32),
             pltpu.VMEM((L, 3 * RANK, HALF), BF16),
@@ -407,21 +399,30 @@
             pltpu.VMEM((L, NX * NY - 1, RANK, BLK), F32),
             pltpu.VMEM((L, NZ, RANK, BLK), F32),
             pltpu.VMEM((L, NBLK, RANK, BLK), F32),
-            pltpu.VMEM((L, RANK, RANK), F32),
+            pltpu.VMEM((L, 3 * RANK, FEATS), BF16),
             pltpu.VMEM((L, NY, 8, COLS), F32),
             pltpu.VMEM((L, NY - 1, 8, COLS), F32),
             pltpu.VMEM((L, NZ, 8, COLS), F32),
-            pltpu.VMEM((L, NY, 8, COLS), F32),
-            pltpu.VMEM((L, RANK, COLS), F32),
-            pltpu.SemaphoreType.DMA((11,)),
-            pltpu.SemaphoreType.DMA((5,)),
+            pltpu.SemaphoreType.DMA((13,)),
         ]
         + [pair] * 18,
         compiler_params=pltpu.CompilerParams(
-            collective_id=0, has_side_effects=True, vmem_limit_bytes=60 * 1024 * 1024
+            collective_id=0, has_side_effects=True, vmem_limit_bytes=50 * 1024 * 1024
         ),
-        cost_estimate=pl.CostEstimate(flops=8_600_000_000, bytes_accessed=39_000_000, transcendentals=0),
+        cost_estimate=pl.CostEstimate(flops=8_400_000_000, bytes_accessed=35_000_000, transcendentals=0),
     )(saved_inputs, kv_cotangent, error_buffer, q_start)
+    return pl.pallas_call(
+        finish,
+        out_shape=(
+            jax.ShapeDtypeStruct((1, L, FEATS, COLS), BF16),
+            jax.ShapeDtypeStruct((L, RANK, COLS), F32),
+        ),
+        in_specs=[vmem_spec] * 4,
+        out_specs=(any_spec, vmem_spec),
+        scratch_shapes=[pltpu.VMEM((L, FEATS, COLS), BF16), pltpu.SemaphoreType.DMA((2 * FEATS // 512,))],
+        compiler_params=pltpu.CompilerParams(vmem_limit_bytes=16 * 1024 * 1024),
+        cost_estimate=pl.CostEstimate(flops=240_000_000, bytes_accessed=4_000_000, transcendentals=0),
+    )(*(pltpu.with_memory_space_constraint(a, pltpu.VMEM) for a in held))
 
 
 def solution(mesh):

time: 70.8 us -> 54.6 us (0.77)
  Pallas kernels: 64.9 us -> 53.3 us
  local copies, waits for them, and re-layouts: 4.78 us -> 0 us
    pallas_call x1 -> x2, Pallas kernels: 64.9 us -> 53.3 us  [the longest x1 50.2 us: body(): pl.pallas_call(kernel, out_shape=(pltpu.VMEM((L, FEATS, COLS), F32), pltp...]
    unnamed x4 -> x0, local copies, waits for them, and re-layouts: 4.78 us -> none
where the time goes in v2:
time: 54.6 us; the launch traced here: 54.1 us
  Pallas kernels  53.3 us (98%)
  between operations  0.8 us (1%)
    pallas_call x1, Pallas kernels, body(): pl.pallas_call(kernel, out_shape=(pltpu.VMEM((L, FEATS, COLS), F32), pltp...  50.2 us
    pallas_call x1, Pallas kernels, body(): pl.pallas_call(finish, out_shape=(jax.ShapeDtypeStruct((1, L, FEATS, COLS...  3.04 us

profile of v2, /device:TPU:8, one launch (start us, length us, event | category | flops | bytes accessed | tf_op | source)
XLA Modules:
  0.0 54.1 jit_solution(9690343438623739384)
XLA Ops:
  0.6 50.2 %shard_map.59 = (f32[2,3584,256]{2,1,0:T(8,128)S(1)}, bf16[2,3584,128]{2,1,0:T(8,128)(2,1)S(1)}, f32[2,32,32]{2,1,0:T(8,128)S(1)}, f32[2,4,8,256]{3,2,1,0:T(8,128)S(1)}) custom-call(bf16[2,2048,3584]{2,1,0:T(8,128)(2,1)} %s_hbm.1, bf16[2,2048,256]{2,1,0:T(8,128)(2,1)} %k_hbm.1, bf16[1,2,3584,256]{3,2,1,0:T(8,128)(2,1)} %e_hbm.1, f32[2,32,256]{2,1,0:T(8,128)} %q_hbm.1), custom_call_target="tpu_custom_call" | custom-call | flops 8400000000 | bytes 35000000 | tf_op jit(solution)/shard_map/pallas_call | solution.py:375
  50.9 3.0 %shard_map.60 = (bf16[1,2,3584,256]{3,2,1,0:T(8,128)(2,1)}, f32[2,32,256]{2,1,0:T(8,128)}) custom-call(f32[2,3584,256]{2,1,0:T(8,128)S(1)} %get-tuple-element.6.m, bf16[2,3584,128]{2,1,0:T(8,128)(2,1)S(1)} %get-tuple-element.7.ot, f32[2,32,32]{2,1,0:T(8,128)S(1)} %get-tuple-element.8.gl, f32[2,4,8,256]{3,2,1,0:T(8,128)S(1)} %get-tuple-element.9.qt), custom_call_target="tpu_custom_call" | custom-call | flops 240000000 | bytes 4000000 | tf_op jit(solution)/shard_map/pallas_call | solution.py:414

commit v3 on v2

v3 whole, which is shorter than its diff:
```python
import functools

import jax
import jax.numpy as jnp
from jax import lax
from jax.experimental import pallas as pl
from jax.experimental.pallas import tpu as pltpu
from jax.sharding import PartitionSpec as P

MESH = pl.DeviceIdType.MESH
F32, BF16 = jnp.float32, jnp.bfloat16
FEATS, RANK, LAYERS, TOK, COLS = 3584, 32, 2, 2048, 256
NZ, NY, NX = 8, 4, 4
HALF = TOK // 2
BLK = 128
NBLK = FEATS // BLK
OWN = NBLK // 2
GRAD_F = 512


def mm(a, b, ca=1, cb=0):
    return lax.dot_general(a, b, (((ca,), (cb,)), ((), ())), preferred_element_type=F32)


def split3(v):
    hi = v.astype(BF16)
    rest = v - hi.astype(F32)
    mid = rest.astype(BF16)
    lo = (rest - mid.astype(F32)).astype(BF16)
    return jnp.concatenate([hi, mid, lo], axis=0)


def fold3(r):
    return r[0:RANK] + r[RANK : 2 * RANK] + r[2 * RANK : 3 * RANK]


SUB = 1
ROWS = RANK // SUB
CUT = 3 * GRAD_F
XY_ORDER = sorted(range(1, NX * NY), key=lambda j: -(min(j % NX, NX - j % NX) + min(j // NX, NY - j // NX)))
Z_ORDER = sorted(range(1, NZ), key=lambda j: -min(j, NZ - j))
Y_ORDER = (2, 1, 3)


def new_error(m, ot, q, rows):
    top = q.astype(BF16)
    rest = (q - top.astype(F32)).astype(BF16)
    return (m[rows, :] - mm(ot[rows, :], jnp.concatenate([top, rest, top, rest], axis=0))).astype(BF16)


def wide_left(v):
    t = split3(v)
    top, mid, low = t[0:RANK], t[RANK : 2 * RANK], t[2 * RANK : 3 * RANK]
    return jnp.concatenate([top, top, top, mid, mid, low], axis=1)


def right_of(top, mid, low):
    return jnp.concatenate([top, mid, low, top, mid, top], axis=0)


def q_from(gl, qt):
    t = split3(jnp.concatenate([qt[i] for i in range(NY)], axis=0))
    return mm(gl[...], right_of(t[0:RANK], t[RANK : 2 * RANK], t[2 * RANK : 3 * RANK]))


def kernel(
    s_hbm, k_hbm, e_hbm, q_hbm, err0, q0, m1, ot1, gl1, qt1,
    s, k, e1, qv, q3, m0, ot0, gl0, qt0, hi, lo, zl, zr, z3, pp, cr, ps, xr, zs, pf, p3, ub, yr, zq,
    hs, z_s, z_r, c_s, c_r, xy_s, xy_r, zz_s, zz_r, ag_s, ag_r, ac_s, ac_r, y1_s, y1_r, qz_s, qz_r, y2_s, y2_r,
):
    e, m, ot, gl, qt = (err0, e1), (m0, m1), (ot0, ot1), (gl0, gl1), (qt0, qt1)
    dp, t = lax.axis_index("dp"), lax.axis_index("tensor")
    z, y, x, c = dp // NY, dp % NY, t // 2, t % 2
    xy = y * NX + x

    def dev(z_, y_, x_, c_):
        return (z_ * NY + y_, x_ * 2 + c_)

    partner = dev(z, y, x, 1 - c)

    def xy_peer(j):
        return (y + j // NX) % NY, (x + j % NX) % NX

    def remote(src, dst, ss, rs, device):
        return pltpu.make_async_remote_copy(
            src_ref=src, dst_ref=dst, send_sem=ss, recv_sem=rs, device_id=device, device_id_type=MESH
        )

    def wait_recv(ref, ss, rs):
        remote(ref, ref, ss, rs, partner).wait_recv()

    def wait_send(ref, ss, rs):
        remote(ref, ref, ss, rs, partner).wait_send()

    barrier = pltpu.get_barrier_semaphore()
    pl.semaphore_signal(barrier, inc=1, device_id=partner, device_id_type=MESH)

    def greet_z(j, _):
        pl.semaphore_signal(barrier, inc=1, device_id=dev((z + j) % NZ, y, x, c), device_id_type=MESH)
        return 0

    def greet_xy(j, _):
        ny, nx = xy_peer(j)
        pl.semaphore_signal(barrier, inc=1, device_id=dev(z, ny, nx, c), device_id_type=MESH)
        return 0

    lax.fori_loop(1, NZ, greet_z, 0)
    lax.fori_loop(1, NX * NY, greet_xy, 0)

    def token_copy(hbm, vmem, l, part, cols, sem):
        rows = pl.ds(pl.multiple_of((c if part == 0 else 1 - c) * HALF, HALF), HALF)
        return pltpu.make_async_copy(hbm.at[l, rows, cols], vmem.at[l, pl.ds(part * HALF, HALF), cols], sem)

    def side_cols(side):
        return pl.ds(pl.multiple_of(side * (FEATS // 2), FEATS // 2), FEATS // 2)

    cq = pltpu.make_async_copy(q_hbm, qv, hs.at[0])
    ck = [[token_copy(k_hbm, k, l, h, pl.ds(0, COLS), hs.at[1 + 2 * l + h]) for h in range(2)] for l in range(LAYERS)]
    ce = [pltpu.make_async_copy(e_hbm.at[0, l], e[l], hs.at[5 + l]) for l in range(LAYERS)]
    own = [
        [token_copy(s_hbm, s, l, 0, side_cols(side), hs.at[7 + 2 * l + i]) for i, side in enumerate((1 - c, c))]
        for l in range(LAYERS)
    ]
    rest = [
        [token_copy(s_hbm, s, l, 1, cols, hs.at[11 + 2 * l + i]) for i, cols in enumerate((pl.ds(0, CUT), pl.ds(CUT, FEATS - CUT)))]
        for l in range(LAYERS)
    ]
    cq.start()
    for l in range(LAYERS):
        ck[l][0].start()
        ck[l][1].start()
    ce[0].start()
    ce[1].start()

    cq.wait()
    for l in range(LAYERS):
        q3[l] = split3(qv[l])
    for l in range(LAYERS):
        ck[l][0].wait()
        ck[l][1].wait()
        own[0][l].start()
        for h in range(2):
            zl[l, h] = fold3(mm(q3[l], k[l, pl.ds(h * HALF, HALF), :], 1, 1))

    def error_part(l):
        ce[l].wait()
        for i in range(4):
            r = fold3(mm(q3[l], e[l][pl.ds(i * 896, 896), :], 1, 1))
            for h in range(SUB):
                for j in range(7):
                    pp[l, h, i * 7 + j] = r[h * ROWS : (h + 1) * ROWS, j * BLK : (j + 1) * BLK]

    error_part(0)
    own[1][0].start()
    error_part(1)

    pl.semaphore_wait(barrier, 1 + (NZ - 1) + (NX * NY - 1))
    for l in range(LAYERS):
        remote(zl.at[l, 1], zr.at[l], z_s.at[l], z_r.at[l], partner).start()

    def p_blocks(l, side):
        for i in range(2):
            b0 = side * OWN + i * 7
            f0 = pl.multiple_of(b0 * BLK, BLK)
            r = fold3(mm(z3[l], s[l, pl.ds(0, HALF), pl.ds(f0, 7 * BLK)]))
            for h in range(SUB):
                for j in range(7):
                    pp[l, h, b0 + j] += r[h * ROWS : (h + 1) * ROWS, j * BLK : (j + 1) * BLK]

    def p_other(l):
        wait_recv(zr.at[l], z_s.at[l], z_r.at[l])
        z3[l] = split3(zl[l, 0] + zr[l])
        own[l][0].wait()
        if l == 0:
            own[1][1].start()
        else:
            rest[0][1].start()
        p_blocks(l, 1 - c)
        for h in range(SUB):
            remote(pp.at[l, h, pl.ds((1 - c) * OWN, OWN)], cr.at[l, h], c_s.at[l, h], c_r.at[l, h], partner).start()

    def p_mine(l):
        own[l][1].wait()
        if l == 0:
            rest[0][0].start()
        else:
            rest[1][0].start()
            rest[1][1].start()
        p_blocks(l, c)

    def mine(l):
        return xy - 2 * l

    def owner(l):
        return (mine(l) >= 0) & (mine(l) < OWN)

    def add_cores(l, h):
        wait_recv(cr.at[l, h], c_s.at[l, h], c_r.at[l, h])
        for b in range(OWN):
            ps[l, h, b] = pp[l, h, c * OWN + b] + cr[l, h, b]
        for j in XY_ORDER:
            ny, nx = xy_peer(j)
            b = ny * NX + nx - 2 * l

            @pl.when((b >= 0) & (b < OWN))
            def _():
                remote(ps.at[l, h, b], xr.at[l, h, j - 1], xy_s.at[l, h], xy_r.at[l, h], dev(z, ny, nx, c)).start()

    def add_plane(l, h):
        @pl.when(owner(l))
        def _():
            wait_recv(xr.at[l, h], xy_s.at[l, h], xy_r.at[l, h])
            total = ps[l, h, mine(l)]
            for j in range(NX * NY - 1):
                total = total + xr[l, h, j]
            zs[l, h, z] = total
            for j in Z_ORDER:
                there = dev((z + j) % NZ, y, x, c)
                remote(zs.at[l, h, z], zs.at[l, h, z], zz_s.at[l, h], zz_r.at[l, h], there).start()

    def add_z(l, h):
        @pl.when(owner(l))
        def _():
            wait_recv(zs.at[l, h, pl.ds(0, NZ - 1)], zz_s.at[l, h], zz_r.at[l, h])
            total = zs[l, h, 0]
            for j in range(1, NZ):
                total = total + zs[l, h, j]
            b = c * OWN + mine(l)
            pf[l, h, b] = total
            for j in XY_ORDER:
                ny, nx = xy_peer(j)
                remote(pf.at[l, h, b], pf.at[l, h, b], ag_s.at[l, h], ag_r.at[l, h], dev(z, ny, nx, c)).start()

    def share_core(l, h):
        @pl.when(owner(l))
        def _():
            wait_recv(pf.at[l, h, pl.ds(0, OWN - 1)], ag_s.at[l, h], ag_r.at[l, h])

        @pl.when(jnp.logical_not(owner(l)))
        def _():
            wait_recv(pf.at[l, h, pl.ds(0, OWN)], ag_s.at[l, h], ag_r.at[l, h])

        half = pf.at[l, h, pl.ds(c * OWN, OWN)]
        remote(half, half, ac_s.at[l, h], ac_r.at[l, h], partner).start()

    def grad(l, i0, i1):
        for i in range(i0, i1):
            rows = pl.ds(i * GRAD_F, GRAD_F)
            if i == 0 or i * GRAD_F == CUT:
                rest[l][0 if i == 0 else 1].wait()
            g = mm(s[l, :, rows], k[l], 0, 0) + e[l][rows, :].astype(F32)
            m[l][rows, :] = g
            top = g.astype(BF16)
            hi[l, rows, :] = top
            lo[l, rows, :] = (g - top.astype(F32)).astype(BF16)

    def q_half(l, side):
        u = jnp.zeros((RANK, COLS), F32)
        for i in range(OWN // 2):
            b0 = side * OWN + 2 * i
            rows = pl.ds(pl.multiple_of(b0 * BLK, 2 * BLK), 2 * BLK)
            halves = [jnp.concatenate([pf[l, h, b0], pf[l, h, b0 + 1]], axis=1) for h in range(SUB)]
            terms = split3(jnp.concatenate(halves, axis=0))
            p3[l, :, rows] = terms
            r = fold3(mm(terms, hi[l, rows, :]))
            r2 = mm(terms[0 : 2 * RANK], lo[l, rows, :])
            u = u + (r + (r2[0:RANK] + r2[RANK : 2 * RANK]))
        return u

    def q_send(l, u):
        for i in range(NY):
            ub[l, i] = u[8 * i : 8 * i + 8]

        for j in Y_ORDER:
            ny = (y + j) % NY
            remote(ub.at[l, ny], yr.at[l, j - 1], y1_s.at[l], y1_r.at[l], dev(z, ny, x, c)).start()

    def q_add_y(l):
        wait_recv(yr.at[l], y1_s.at[l], y1_r.at[l])
        zq[l, z] = ub[l, y] + yr[l, 0] + yr[l, 1] + yr[l, 2]
        for j in Z_ORDER:
            remote(zq.at[l, z], zq.at[l, z], qz_s.at[l], qz_r.at[l], dev((z + j) % NZ, y, x, c)).start()

    def q_add_z(l):
        wait_recv(zq.at[l, pl.ds(0, NZ - 1)], qz_s.at[l], qz_r.at[l])
        total = zq[l, 0]
        for j in range(1, NZ):
            total = total + zq[l, j]
        qt[l][y] = total * (1.0 / (NZ * NY))
        for j in Y_ORDER:
            remote(qt[l].at[y], qt[l].at[y], y2_s.at[l], y2_r.at[l], dev(z, (y + j) % NY, x, c)).start()

    def gram(l):
        g = jnp.zeros((3 * RANK, 3 * RANK), F32)
        for i in range(FEATS // 512):
            terms = p3[l, :, pl.ds(i * 512, 512)]
            g = g + mm(terms, terms, 1, 1)
        g = fold3(g)
        return g[:, 0:RANK] + g[:, RANK : 2 * RANK] + g[:, 2 * RANK : 3 * RANK]

    def inverse_factors(grams):
        rows = lax.broadcasted_iota(jnp.int32, (RANK, 1), 0)
        eye = (rows == lax.broadcasted_iota(jnp.int32, (RANK, RANK), 1)).astype(F32)
        work = [jnp.concatenate([g, eye], axis=1) for g in grams]
        for j in range(RANK):
            for n, a in enumerate(work):
                inv = lax.rsqrt(a[j : j + 1, j : j + 1])
                row = a[j : j + 1, :] * inv
                col = jnp.where(rows > j, a[:, j : j + 1] * inv, 0.0)
                work[n] = jnp.where(rows == j, row, a - col * row)
        return [a[:, RANK : 2 * RANK] for a in work]

    def ortho(l):
        for i in range(FEATS // 512):
            rows = pl.ds(i * 512, 512)
            o = mm(gl[l][...], right_of(*(p3[l, pl.ds(n * RANK, RANK), rows] for n in range(3))))
            o_top = o.astype(BF16)
            o_low = (o - o_top.astype(F32)).astype(BF16)
            ot[l][rows, :] = jnp.concatenate([o_top, o_top, o_low, o_low], axis=0).T

    pairs = [(l, h) for l in range(LAYERS) for h in range(SUB)]
    for l in range(LAYERS):
        p_other(l)
        p_mine(l)
        for h in range(SUB):
            add_cores(l, h)
    grad(0, 0, 5)
    for l, h in pairs:
        add_plane(l, h)
    grad(0, 5, 7)
    grad(1, 0, 3)
    for l, h in pairs:
        add_z(l, h)
    grad(1, 3, 7)
    for l, h in pairs:
        share_core(l, h)
    own_q = [q_half(l, c) for l in range(LAYERS)]
    for l in range(LAYERS):
        for h in range(SUB):
            wait_recv(pf.at[l, h, pl.ds(0, OWN)], ac_s.at[l, h], ac_r.at[l, h])
        q_send(l, own_q[l] + q_half(l, 1 - c))
    grams = [gram(l) for l in range(LAYERS)]
    for l in range(LAYERS):
        q_add_y(l)
    for l, inverse in enumerate(inverse_factors(grams)):
        gl[l][...] = wide_left(inverse)
    for l in range(LAYERS):
        q_add_z(l)
    ortho(0)
    ortho(1)
    wait_recv(qt[0].at[pl.ds(0, NY - 1)], y2_s.at[0], y2_r.at[0])
    q0[...] = q_from(gl[0], qt[0])
    for i in range(FEATS // 512):
        rows = pl.ds(i * 512, 512)
        err0[rows, :] = new_error(m[0], ot[0], q0[...], rows)
    wait_recv(qt[1].at[pl.ds(0, NY - 1)], y2_s.at[1], y2_r.at[1])

    for l in range(LAYERS):
        wait_send(zl.at[l, 1], z_s.at[l], z_r.at[l])
        for h in range(SUB):
            wait_send(cr.at[l, h], c_s.at[l, h], c_r.at[l, h])

            @pl.when(owner(l))
            def _():
                wait_send(ps.at[l, h, pl.ds(0, OWN - 1)], xy_s.at[l, h], xy_r.at[l, h])
                wait_send(zs.at[l, h, pl.ds(0, NZ - 1)], zz_s.at[l, h], zz_r.at[l, h])
                wait_send(pf.at[l, h, pl.ds(0, NX * NY - 1)], ag_s.at[l, h], ag_r.at[l, h])

            @pl.when(jnp.logical_not(owner(l)))
            def _():
                wait_send(ps.at[l, h, pl.ds(0, OWN)], xy_s.at[l, h], xy_r.at[l, h])

            wait_send(pf.at[l, h, pl.ds(0, OWN)], ac_s.at[l, h], ac_r.at[l, h])
        wait_send(ub.at[l, pl.ds(0, NY - 1)], y1_s.at[l], y1_r.at[l])
        wait_send(zq.at[l, pl.ds(0, NZ - 1)], qz_s.at[l], qz_r.at[l])
        wait_send(qt[l].at[pl.ds(0, NY - 1)], y2_s.at[l], y2_r.at[l])


def finish(err0, q0, m1, ot1, gl1, qt1, err_hbm, qf, out, sems):
    first = pltpu.make_async_copy(err0, err_hbm.at[0, 0], sems.at[0])
    first.start()
    copies = [first]
    q = q_from(gl1, qt1)
    qf[0] = q0[...]
    qf[1] = q
    for i in range(FEATS // 512):
        rows = pl.ds(i * 512, 512)
        out[rows, :] = new_error(m1, ot1, q, rows)
        copies.append(pltpu.make_async_copy(out.at[rows], err_hbm.at[0, 1, rows], sems.at[1 + i]))
        copies[-1].start()
    for copy in copies:
        copy.wait()


def body(saved_inputs, kv_cotangent, error_buffer, q_start):
    L = LAYERS
    pair, four = pltpu.SemaphoreType.DMA((L,)), pltpu.SemaphoreType.DMA((L, SUB))
    any_spec, vmem_spec = pl.BlockSpec(memory_space=pl.ANY), pl.BlockSpec(memory_space=pltpu.VMEM)
    held = pl.pallas_call(
        kernel,
        out_shape=(
            pltpu.VMEM((FEATS, COLS), BF16),
            pltpu.VMEM((RANK, COLS), F32),
            pltpu.VMEM((FEATS, COLS), F32),
            pltpu.VMEM((FEATS, 128), BF16),
            pltpu.VMEM((RANK, 6 * RANK), BF16),
            pltpu.VMEM((NY, 8, COLS), F32),
        ),
        in_specs=[any_spec] * 4,
        out_specs=(vmem_spec,) * 6,
        scratch_shapes=[
            pltpu.VMEM((L, TOK, FEATS), BF16),
            pltpu.VMEM((L, TOK, COLS), BF16),
            pltpu.VMEM((FEATS, COLS), BF16),
            pltpu.VMEM((L, RANK, COLS), F32),
            pltpu.VMEM((L, 3 * RANK, COLS), BF16),
            pltpu.VMEM((FEATS, COLS), F32),
            pltpu.VMEM((FEATS, 128), BF16),
            pltpu.VMEM((RANK, 6 * RANK), BF16),
            pltpu.VMEM((NY, 8, COLS), F32),
            pltpu.VMEM((L, FEATS, COLS), BF16),
            pltpu.VMEM((L, FEATS, COLS), BF16),
            pltpu.VMEM((L, 2, RANK, HALF), F32),
            pltpu.VMEM((L, RANK, HALF), F32),
            pltpu.VMEM((L, 3 * RANK, HALF), BF16),
            pltpu.VMEM((L, SUB, NBLK, ROWS, BLK), F32),
            pltpu.VMEM((L, SUB, OWN, ROWS, BLK), F32),
            pltpu.VMEM((L, SUB, OWN, ROWS, BLK), F32),
            pltpu.VMEM((L, SUB, NX * NY - 1, ROWS, BLK), F32),
            pltpu.VMEM((L, SUB, NZ, ROWS, BLK), F32),
            pltpu.VMEM((L, SUB, NBLK, ROWS, BLK), F32),
            pltpu.VMEM((L, 3 * RANK, FEATS), BF16),
            pltpu.VMEM((L, NY, 8, COLS), F32),
            pltpu.VMEM((L, NY - 1, 8, COLS), F32),
            pltpu.VMEM((L, NZ, 8, COLS), F32),
            pltpu.SemaphoreType.DMA((15,)),
        ]
        + [pair] * 2
        + [four] * 10
        + [pair] * 6,
        compiler_params=pltpu.CompilerParams(
            collective_id=0, has_side_effects=True, vmem_limit_bytes=54 * 1024 * 1024
        ),
        cost_estimate=pl.CostEstimate(flops=8_400_000_000, bytes_accessed=35_000_000, transcendentals=0),
    )(saved_inputs, kv_cotangent, error_buffer, q_start)
    return pl.pallas_call(
        finish,
        out_shape=(
            jax.ShapeDtypeStruct((1, L, FEATS, COLS), BF16),
            jax.ShapeDtypeStruct((L, RANK, COLS), F32),
        ),
        in_specs=[vmem_spec] * 6,
        out_specs=(any_spec, vmem_spec),
        scratch_shapes=[pltpu.VMEM((FEATS, COLS), BF16), pltpu.SemaphoreType.DMA((1 + FEATS // 512,))],
        compiler_params=pltpu.CompilerParams(vmem_limit_bytes=16 * 1024 * 1024),
        cost_estimate=pl.CostEstimate(flops=240_000_000, bytes_accessed=4_000_000, transcendentals=0),
    )(*(pltpu.with_memory_space_constraint(a, pltpu.VMEM) for a in held))


def solution(mesh):
    placed = (
        P(None, "dp", None),
        P(None, "dp", "tensor"),
        P("dp", None, None, "tensor"),
        P(None, None, "tensor"),
    )
    return jax.shard_map(
        body,
        mesh=mesh,
        in_specs=placed,
        out_specs=(P("dp", None, None, "tensor"), P(None, None, "tensor")),
        check_vma=False,
    )
```

time: 54.6 us -> 53.4 us (0.978)
  Pallas kernels: 53.3 us -> 52.5 us
where the time goes in v3:
time: 53.4 us; the launch traced here: 53.3 us
  Pallas kernels  52.5 us (98%)
  between operations  0.8 us (1%)
    pallas_call x1, Pallas kernels, body(): pl.pallas_call(kernel, out_shape=(pltpu.VMEM((FEATS, COLS), BF16), pltpu....  49.9 us
    pallas_call x1, Pallas kernels, body(): pl.pallas_call(finish, out_shape=(jax.ShapeDtypeStruct((1, L, FEATS, COLS...  2.55 us

profile of v3, /device:TPU:8, one launch (start us, length us, event | category | flops | bytes accessed | tf_op | source)
XLA Modules:
  0.0 53.3 jit_solution(11828533718492570451)
XLA Ops:
  0.6 49.9 %shard_map.59 = (bf16[3584,256]{1,0:T(8,128)(2,1)S(1)}, f32[32,256]{1,0:T(8,128)S(1)}, f32[3584,256]{1,0:T(8,128)S(1)}, bf16[3584,128]{1,0:T(8,128)(2,1)S(1)}, b...) custom-call(bf16[2,2048,3584]{2,1,0:T(8,128)(2,1)} %s_hbm.1, bf16[2,2048,256]{2,1,0:T(8,128)(2,1)} %k_hbm.1, ...), custom_call_target="tpu_custom_call" | custom-call | flops 8400000000 | bytes 35000000 | tf_op jit(solution)/shard_map/pallas_call | solution.py:399
  50.6 2.6 %shard_map.60 = (bf16[1,2,3584,256]{3,2,1,0:T(8,128)(2,1)}, f32[2,32,256]{2,1,0:T(8,128)}) custom-call(bf16[3584,256]{1,0:T(8,128)(2,1)S(1)} %get-tuple-element.8.err0, f32[32,256]{1,0:T(8,128)S(1)} %get-tuple-element.9.q0, f32[3584,256]{1,0:T(8,128)S(1)} %get-tuple-element.10.m1, bf16[3584,128]{1,0:T(8,128)(2,1)S(1)} %get-tuple-element.11.ot1, ...), custom_call_target="tpu_custom_call" | custom-call | flops 240000000 | bytes 4000000 | tf_op jit(solution)/shard_map/pallas_call | solution.py:446

commit v4 on v3

--- a/solution.py
+++ b/solution.py
@@ -171,21 +171,17 @@
         wait_recv(zr.at[l], z_s.at[l], z_r.at[l])
         z3[l] = split3(zl[l, 0] + zr[l])
         own[l][0].wait()
+        p_blocks(l, 1 - c)
+        for h in range(SUB):
+            remote(pp.at[l, h, pl.ds((1 - c) * OWN, OWN)], cr.at[l, h], c_s.at[l, h], c_r.at[l, h], partner).start()
+
+    def p_mine(l):
+        own[l][1].wait()
         if l == 0:
             own[1][1].start()
         else:
+            rest[0][0].start()
             rest[0][1].start()
-        p_blocks(l, 1 - c)
-        for h in range(SUB):
-            remote(pp.at[l, h, pl.ds((1 - c) * OWN, OWN)], cr.at[l, h], c_s.at[l, h], c_r.at[l, h], partner).start()
-
-    def p_mine(l):
-        own[l][1].wait()
-        if l == 0:
-            rest[0][0].start()
-        else:
-            rest[1][0].start()
-            rest[1][1].start()
         p_blocks(l, c)
 
     def mine(l):
@@ -247,7 +243,10 @@
         for i in range(i0, i1):
             rows = pl.ds(i * GRAD_F, GRAD_F)
             if i == 0 or i * GRAD_F == CUT:
-                rest[l][0 if i == 0 else 1].wait()
+                part = 0 if i == 0 else 1
+                rest[l][part].wait()
+                if l == 0:
+                    rest[1][part].start()
             g = mm(s[l, :, rows], k[l], 0, 0) + e[l][rows, :].astype(F32)
             m[l][rows, :] = g
             top = g.astype(BF16)
@@ -376,17 +375,19 @@
         wait_send(qt[l].at[pl.ds(0, NY - 1)], y2_s.at[l], y2_r.at[l])
 
 
-def finish(err0, q0, m1, ot1, gl1, qt1, err_hbm, qf, out, sems):
+def finish(err0, q0, m1, ot1, gl1, qt1, err_hbm, qf_hbm, out, qf, sems):
     first = pltpu.make_async_copy(err0, err_hbm.at[0, 0], sems.at[0])
     first.start()
     copies = [first]
     q = q_from(gl1, qt1)
     qf[0] = q0[...]
     qf[1] = q
+    copies.append(pltpu.make_async_copy(qf, qf_hbm, sems.at[1]))
+    copies[-1].start()
     for i in range(FEATS // 512):
         rows = pl.ds(i * 512, 512)
         out[rows, :] = new_error(m1, ot1, q, rows)
-        copies.append(pltpu.make_async_copy(out.at[rows], err_hbm.at[0, 1, rows], sems.at[1 + i]))
+        copies.append(pltpu.make_async_copy(out.at[rows], err_hbm.at[0, 1, rows], sems.at[2 + i]))
         copies[-1].start()
     for copy in copies:
         copy.wait()
@@ -450,8 +451,12 @@
             jax.ShapeDtypeStruct((L, RANK, COLS), F32),
         ),
         in_specs=[vmem_spec] * 6,
-        out_specs=(any_spec, vmem_spec),
-        scratch_shapes=[pltpu.VMEM((FEATS, COLS), BF16), pltpu.SemaphoreType.DMA((1 + FEATS // 512,))],
+        out_specs=(any_spec, any_spec),
+        scratch_shapes=[
+            pltpu.VMEM((FEATS, COLS), BF16),
+            pltpu.VMEM((L, RANK, COLS), F32),
+            pltpu.SemaphoreType.DMA((2 + FEATS // 512,)),
+        ],
         compiler_params=pltpu.CompilerParams(vmem_limit_bytes=16 * 1024 * 1024),
         cost_estimate=pl.CostEstimate(flops=240_000_000, bytes_accessed=4_000_000, transcendentals=0),
     )(*(pltpu.with_memory_space_constraint(a, pltpu.VMEM) for a in held))

time: 53.4 us -> 52.8 us (0.989)
  Pallas kernels: 52.5 us -> 51.9 us
    pallas_call x1, Pallas kernels: 2.55 us -> 1.93 us  [body(): pl.pallas_call(finish, out_shape=(jax.ShapeDtypeStruct((1, L, FEATS, COLS...]
where the time goes in v4:
time: 52.8 us; the launch traced here: 52.7 us
  Pallas kernels  51.9 us (98%)
  between operations  0.8 us (2%)
    pallas_call x1, Pallas kernels, body(): pl.pallas_call(kernel, out_shape=(pltpu.VMEM((FEATS, COLS), BF16), pltpu....  50 us
    pallas_call x1, Pallas kernels, body(): pl.pallas_call(finish, out_shape=(jax.ShapeDtypeStruct((1, L, FEATS, COLS...  1.93 us

profile of v4, /device:TPU:8, one launch (start us, length us, event | category | flops | bytes accessed | tf_op | source)
XLA Modules:
  0.0 52.7 jit_solution(1239134755324558672)
XLA Ops:
  0.6 50.0 %shard_map.59 = (bf16[3584,256]{1,0:T(8,128)(2,1)S(1)}, f32[32,256]{1,0:T(8,128)S(1)}, f32[3584,256]{1,0:T(8,128)S(1)}, bf16[3584,128]{1,0:T(8,128)(2,1)S(1)}, b...) custom-call(bf16[2,2048,3584]{2,1,0:T(8,128)(2,1)} %s_hbm.1, bf16[2,2048,256]{2,1,0:T(8,128)(2,1)} %k_hbm.1, ...), custom_call_target="tpu_custom_call" | custom-call | flops 8400000000 | bytes 35000000 | tf_op jit(solution)/shard_map/pallas_call | solution.py:400
  50.6 1.9 %shard_map.60 = (bf16[1,2,3584,256]{3,2,1,0:T(8,128)(2,1)}, f32[2,32,256]{2,1,0:T(8,128)}) custom-call(bf16[3584,256]{1,0:T(8,128)(2,1)S(1)} %get-tuple-element.8.err0, f32[32,256]{1,0:T(8,128)S(1)} %get-tuple-element.9.q0, f32[3584,256]{1,0:T(8,128)S(1)} %get-tuple-element.10.m1, bf16[3584,128]{1,0:T(8,128)(2,1)S(1)} %get-tuple-element.11.ot1, ...), custom_call_target="tpu_custom_call" | custom-call | flops 240000000 | bytes 4000000 | tf_op jit(solution)/shard_map/pallas_call | solution.py:447
